TPU v7x, 256 devices: a whole 4x4x8 slice. The times are simulated.
256 devices in a mesh: occ: 32 (over y_lo, z, core), aux: 4 (over x), vir: 2 (over y_hi).
Axes of the slice: x: 4, y: 4 (y_hi: 2, y_lo: 2; y = y_hi * 2 + y_lo), z: 8, core: 2. Of those that a mesh axis runs over, the one named last changes fastest.
Arguments:
- integrals: bfloat16 [32, 2048, 4096], P('occ', 'vir', 'aux'), may hold values from -0.65625 to 0.65625
- occ_energy: float32 [32], replicated, may hold values from -2 to -0.5
- vir_energy: float32 [2048], replicated, may hold values from 0.25 to 3
Outputs:
- lagrangian: bfloat16 [32, 2048, 4096], P('occ', 'vir', 'aux')
All inputs are finite; a program needn't handle non-finite values.
Results may differ from a plain program's by a relative error of at most 0.0039.
Values may be sent and summed in bfloat16 or wider, within the bound.
A program may use at most 64 MiB of HBM per device.

v0:
```python
import jax
import jax.numpy as jnp
from jax import lax
from jax.sharding import PartitionSpec as P


def shifted_2(value, axis, by):
    count = lax.axis_size(axis)
    return lax.ppermute(value, axis, [(i, (i + by) % count) for i in range(count)])


def on_device(integrals, occ_energy, vir_energy):
    row_count = integrals.shape[0]
    vir_width = integrals.shape[1]
    cycle_size = lax.axis_size("occ")
    position = lax.axis_index("occ")
    own_level = lax.dynamic_slice_in_dim(occ_energy, position * row_count, row_count)
    partner_level = lax.dynamic_slice_in_dim(
        occ_energy, (position - 2) % cycle_size * row_count, row_count
    )
    local_vir = lax.dynamic_slice_in_dim(vir_energy, lax.axis_index("vir") * vir_width, vir_width)
    shifted = shifted_2(integrals, "occ", 2)
    partner = lax.all_gather(shifted, "vir", axis=1, tiled=True)
    virtuals = partner.shape[1]
    pair_level = own_level + partner_level
    share_rows = virtuals // lax.axis_size("aux")
    partner_cols = partner
    partial_value = lax.psum_scatter(
        jnp.einsum("nbq,naq->bna", partner_cols, integrals, preferred_element_type=jnp.float32),
        "aux",
        scatter_dimension=0,
        tiled=True,
    )
    first_row = lax.axis_index("aux") * share_rows
    vir_rows = lax.dynamic_slice_in_dim(vir_energy, first_row, share_rows)
    amplitudes = (
        partial_value
        / (pair_level[None, :, None] - vir_rows[:, None, None] - local_vir[None, None, :])
    ).astype(jnp.bfloat16)
    portion = lax.all_gather(amplitudes, "aux", axis=0, tiled=True)
    partner_cols = partner
    own_part = jnp.einsum("bna,nbq->naq", portion, partner_cols, preferred_element_type=jnp.float32)
    rows_back = jnp.einsum("bna,naq->nbq", portion, integrals, preferred_element_type=jnp.float32)
    own_part, second_part = (own_part, rows_back)
    owned = lax.psum_scatter(second_part, "vir", scatter_dimension=1, tiled=True)
    returned = shifted_2(owned, "occ", -2)
    return (own_part + returned).astype(jnp.bfloat16)


def solution(mesh):
    placed = (P("occ", "vir", "aux"), P(), P())
    return jax.shard_map(
        on_device, mesh=mesh, in_specs=placed, out_specs=P("occ", "vir", "aux"), check_vma=False
    )
```

profile of v0, /device:TPU:225, one launch (start us, length us, event | category | flops | bytes accessed | tf_op | source)
XLA Modules:
  0.0 492.6 jit_solution(18041333960076744239)
XLA Ops:
  6.5 0.0 all-gather.3.cloned.1.call-start
  6.5 0.0 collective-permute-start
  6.5 46.7 %collective-permute-done = bf16[1,1024,1024]{2,1,0:T(8,128)(2,1)S(1)} collective-permute-done((bf16[1,1024,1024]{2,1,0:T(8,128)(2,1)}, bf16[1,1024,1024]{2,1,0:T(8,128)(2,1)S(1)}, u32[]{:S(2)}, u32[]{:S(2)}) %collective-permute-start) | collective-permute-done | bytes 2097184 | tf_op jit(solution)/shard_map/ppermute | solution.py:9
  53.2 0.0 copy-start
  53.2 1.3 copy-done
  54.6 0.0 all-gather.3.cloned.1.call-update
  54.6 0.0 reduce-scatter.3.cloned.1.call-start
  54.6 66.0 %all-gather.3.cloned.1.call-done = bf16[1,2048,1024]{2,1,0:T(8,128)(2,1)} async-done(((bf16[1,1024,1024]{2,1,0:T(8,128)(2,1)}), bf16[1,2048,1024]{2,1,0:T(8,128)(2,1)}) %all-gather.3.cloned.1.call-update) | async-done | bytes 4194320 | tf_op jit(solution)/shard_map/all_gather | solution.py:23
  120.6 10.6 %convolution_bitcast_fusion.1 = f32[2048,1,1024]{0,2,1:T(8,128)} fusion(bf16[1,2048,1024]{2,1,0:T(8,128)(2,1)} %all-gather.3.cloned.1.call-done, bf16[1,1024,1024]{2,1,0:T(8,128)(2,1)} %param.3), kind=kOutput, calls=%fused_computation.1 | convolution fusion | flops 4294967296 | bytes 14680064 | tf_op jit(solution)/shard_map/nbq,naq->bna/dot_general | solution.py:29
  131.2 0.0 copy-start.2
  131.2 0.0 copy-start.1
  131.2 0.0 reduce-scatter.3.cloned.1.call-update
  131.2 0.0 copy-start.3
  131.2 0.0 all-gather.5.cloned.1.call-start
  131.3 0.5 copy-done.2
  131.9 0.7 fusion.12
  133.8 0.0 copy-done.1
  133.8 0.1 dynamic-slice_subtract_fusion
  133.9 80.0 %reduce-scatter.3.cloned.1.call-done = f32[512,1,1024]{0,2,1:T(8,128)} async-done(((f32[2048,1,1024]{0,2,1:T(8,128)}), f32[512,1,1024]{0,2,1:T(8,128)}) %reduce-scatter.3.cloned.1.call-update) | async-done | bytes 2097168 | tf_op jit(solution)/shard_map/reduce_scatter | solution.py:28
  213.9 2.9 divide_convert_fusion
  216.8 0.0 all-gather.5.cloned.1.call-update
  216.8 0.0 reduce-scatter.5.cloned.1.call-start
  216.9 50.6 %all-gather.5.cloned.1.call-done = bf16[2048,1,1024]{0,2,1:T(8,128)(2,1)} async-done(((bf16[512,1,1024]{0,2,1:T(8,128)(2,1)}), bf16[2048,1,1024]{0,2,1:T(8,128)(2,1)}) %all-gather.5.cloned.1.call-update) | async-done | bytes 4194320 | tf_op jit(solution)/shard_map/all_gather | solution.py:40
  267.5 0.0 copy-done.3
  267.5 9.1 %convolution_bitcast_fusion = f32[1,2048,1024]{2,1,0:T(8,128)} fusion(bf16[2048,1,1024]{0,2,1:T(8,128)(2,1)} %all-gather.5.cloned.1.call-done, bf16[1,1024,1024]{2,1,0:T(8,128)(2,1)S(1)} %copy-done.3), kind=kOutput, calls=%fused_computation | convolution fusion | flops 4294967296 | bytes 14680064 | tf_op jit(solution)/shard_map/bna,naq->nbq/dot_general | solution.py:43
  276.5 0.0 reduce-scatter.5.cloned.1.call-update
  276.5 106.4 %reduce-scatter.5.cloned.1.call-done = f32[1,1024,1024]{2,1,0:T(8,128)} async-done(((f32[1,2048,1024]{2,1,0:T(8,128)}), f32[1,1024,1024]{2,1,0:T(8,128)}) %reduce-scatter.5.cloned.1.call-update) | async-done | bytes 4194320 | tf_op jit(solution)/shard_map/reduce_scatter | solution.py:45
  383.0 1.1 collective-permute-start.1
  384.1 92.6 %collective-permute-done.1 = f32[1,1024,1024]{2,1,0:T(8,128)S(1)} collective-permute-done((f32[1,1024,1024]{2,1,0:T(8,128)}, f32[1,1024,1024]{2,1,0:T(8,128)S(1)}, u32[]{:S(2)}, u32[]{:S(2)}) %collective-permute-start.1) | collective-permute-done | bytes 4194336 | tf_op jit(solution)/shard_map/ppermute | solution.py:9
  476.7 9.3 %fusion = bf16[1,1024,1024]{2,1,0:T(8,128)(2,1)} fusion(f32[1,1024,1024]{2,1,0:T(8,128)S(1)} %collective-permute-done.1, bf16[1,2048,1024]{2,1,0:T(8,128)(2,1)} %all-gather.3.cloned.1.call-done, bf16[2048,1,1024]{0,2,1:T(8,128)(2,1)} %all-gather.5.cloned.1.call-done), kind=kOutput, calls=%fused_computation.3 | convolution fusion | flops 4297064448 | bytes 14680064 | tf_op jit(solution)/shard_map/bna,nbq->naq/dot_general | solution.py:42
  (1 shorter events, 0.0 us)
Async XLA Ops:
  6.5 114.1 %all-gather.3.cloned.1.call-start = ((), (), s32[]{:S(2)}) async-start(), calls=%async_computation.2 | async-start | bytes 6291456 | tf_op jit(solution)/shard_map/all_gather | solution.py:23
  6.5 46.7 %collective-permute-start = (bf16[1,1024,1024]{2,1,0:T(8,128)(2,1)}, bf16[1,1024,1024]{2,1,0:T(8,128)(2,1)S(1)}, u32[]{:S(2)}, u32[]{:S(2)}) collective-permute-start(bf16[1,1024,1024]{2,1,0:T(8,128)(2,1)} %param.3), channel_id=1, source_target_pairs={{0,16},{8,24},{16,32},{24,40},{32,48},{40,56},{48,64},{56,72},{64,... | collective-permute-start | bytes 6291464 | tf_op jit(solution)/shard_map/ppermute | solution.py:9
  53.2 1.3 copy-start
  54.6 159.3 %reduce-scatter.3.cloned.1.call-start = ((), (), s32[]{:S(2)}) async-start(), calls=%async_computation.3 | async-start | bytes 10485760 | tf_op jit(solution)/shard_map/reduce_scatter | solution.py:28
  131.2 0.7 copy-start.2
  131.2 2.6 copy-start.1
  131.2 136.2 %copy-start.3 = (bf16[1,1024,1024]{2,1,0:T(8,128)(2,1)S(1)}, bf16[1,1024,1024]{2,1,0:T(8,128)(2,1)}, u32[]{:S(2)}) copy-start(bf16[1,1024,1024]{2,1,0:T(8,128)(2,1)} %param.3) | copy-start | bytes 6291460
  131.2 136.2 %all-gather.5.cloned.1.call-start = ((), (), s32[]{:S(2)}) async-start(), calls=%async_computation.4 | async-start | bytes 5242880 | tf_op jit(solution)/shard_map/all_gather | solution.py:40
  216.8 166.1 %reduce-scatter.5.cloned.1.call-start = ((), (), s32[]{:S(2)}) async-start(), calls=%async_computation.5 | async-start | bytes 12582912 | tf_op jit(solution)/shard_map/reduce_scatter | solution.py:45
  383.0 93.7 %collective-permute-start.1 = (f32[1,1024,1024]{2,1,0:T(8,128)}, f32[1,1024,1024]{2,1,0:T(8,128)S(1)}, u32[]{:S(2)}, u32[]{:S(2)}) collective-permute-start(f32[1,1024,1024]{2,1,0:T(8,128)} %reduce-scatter.5.cloned.1.call-done), channel_id=1, source_target_pairs={{0,240},{8,248},{16,0},{24,8},{32,16},{40,24},{48,32},{56,40},{64,... | collective-permute-start | bytes 12582920 | tf_op jit(solution)/shard_map/ppermute | solution.py:9
Sparse Core Ops, SparseCore 0:
  54.7 65.8 all-gather.2
  131.4 82.4 reduce-scatter.2
  217.0 50.4 all-gather.4
  276.7 106.2 reduce-scatter.4
where the time goes:
time: 495 us; the launch traced here: 493 us
  waiting for transfers between devices  442 us (89%)
  matrix products  29 us (6%)
  between operations  14.5 us (3%)
    ppermute x2, waiting for transfers between devices, shifted_2(): lax.ppermute(value, axis, [(i, (i + by) % count) for i in range(count)])  139 us
    reduce_scatter x1, waiting for transfers between devices, on_device(): lax.psum_scatter(second_part, 'vir', scatter_dimension=1, tiled=True)  106 us
    reduce_scatter x1, waiting for transfers between devices, on_device(): lax.psum_scatter(jnp.einsum('nbq,naq->bna', partner_cols, integrals, pref...  80 us
    all_gather x1, waiting for transfers between devices, on_device(): partner = lax.all_gather(shifted, 'vir', axis=1, tiled=True)  66 us
    all_gather x1, waiting for transfers between devices, on_device(): portion = lax.all_gather(amplitudes, 'aux', axis=0, tiled=True)  50.6 us
    dot_general x1, matrix products, on_device(): jnp.einsum('nbq,naq->bna', partner_cols, integrals, preferred_element_typ...  10.6 us
  transfers between devices with their start and end apart: 6, of which 6 were waited for; matrix products, arithmetic and copies ran while one was open for 0% of the time, Pallas kernels for 0%

commit v1 on v0

v1 whole, which is shorter than its diff:
```python
import functools

import jax
import jax.numpy as jnp
from jax import lax
from jax.experimental import pallas as pl
from jax.experimental.pallas import tpu as pltpu
from jax.sharding import PartitionSpec as P

MESH = pl.DeviceIdType.MESH
BF16 = jnp.bfloat16
F32 = jnp.float32

K = 4
R = 256
W = 2 * R
S = R // 4
H = S // 2
SLOTS = 4

TILES = [(0, 0)]
for k in range(1, K):
    for j in range(k):
        TILES += [(k, j), (j, k)]
    TILES += [(k, k)]
NT = len(TILES)
ROW_END = {a: max(t for t, tile in enumerate(TILES) if tile[0] == a) for a in range(K)}
COL_END = {b: max(t for t, tile in enumerate(TILES) if tile[1] == b) for b in range(K)}

OFF = {"A": 0, "B": 1, "C": 2, "D": 3, "E": 4}


def kernel(
    x_ref, acol_ref, brow_ref, out_ref,
    bi, bp, vf, s1, s2, r1, r2, tt, own, back, cr, zs, zr, os_,
    in_s, in_r, zi_s, zi_r, ci_s, ci_r, x_s, x_r, cb_s, cb_r, zb_s, zb_r, o_s, o_r,
):
    o, x, v = lax.axis_index("occ"), lax.axis_index("aux"), lax.axis_index("vir")
    c = lax.rem(o, 2)
    cross = c + v == 1
    straight = c + v != 1
    flip = o + 1 - 2 * c
    xp = (o, lax.rem(x + 1, 4), v)
    xm = (o, lax.rem(x + 3, 4), v)
    zp = (lax.rem(o + 2, 32), x, v)
    zm = (lax.rem(o + 30, 32), x, v)
    core = (flip, x, v)
    swap = (flip, x, 1 - v)

    def remote(src, dst, ssem, rsem, to):
        return pltpu.make_async_remote_copy(
            src_ref=src, dst_ref=dst, send_sem=ssem, recv_sem=rsem, device_id=to, device_id_type=MESH
        )

    barrier = pltpu.get_barrier_semaphore()
    for peer in (xp, xm, zp, zm, core, swap):
        pl.semaphore_signal(barrier, inc=1, device_id=peer, device_id_type=MESH)
    pl.semaphore_wait(barrier, 6)

    def rows(k):
        return pl.ds(k * R, R)

    def in_remote(k):
        return remote(x_ref.at[rows(k)], bi.at[k], in_s.at[k], in_r.at[k], swap)

    def in_local(k):
        return pltpu.make_async_copy(x_ref.at[rows(k)], bi.at[k], in_r.at[k])

    def out_remote(k):
        return remote(os_.at[k], out_ref.at[rows(k)], o_s.at[k], o_r.at[k], swap)

    def out_local(k):
        return pltpu.make_async_copy(os_.at[k], out_ref.at[rows(k)], o_r.at[k])

    def z_in(k):
        return remote(bi.at[k], bp.at[0, k], zi_s.at[k], zi_r.at[k], zp)

    def c_in(k):
        return remote(bp.at[0, k], bp.at[1, k], ci_s.at[k], ci_r.at[k], core)

    def c_back(k):
        return remote(back.at[1, k], cr.at[k], cb_s.at[k], cb_r.at[k], core)

    def z_back(k):
        return remote(zs.at[k], zr.at[k], zb_s.at[k], zb_r.at[k], zm)

    far = lax.rem(x + 2, 4)
    low = lax.rem(x + 3, 4)
    high = lax.rem(x + 1, 4)

    def part(shard, first, count):
        return pl.ds(pl.multiple_of(shard * S + first, H), count)

    def rs1(t):
        return (
            remote(s1.at[t, pl.ds(0, H)], r1.at[t, 0], x_s.at[0, t], x_r.at[0, t], xm),
            remote(s1.at[t, pl.ds(H, H)], r1.at[t, 1], x_s.at[1, t], x_r.at[1, t], xp),
        )

    def rs2(t):
        return (
            remote(s2.at[t, 0], r2.at[t, 0], x_s.at[2, t], x_r.at[2, t], xm),
            remote(s2.at[t, 1], r2.at[t, 1], x_s.at[3, t], x_r.at[3, t], xp),
        )

    def ag1(t):
        mine = tt.at[t, part(x, 0, S)]
        return (
            remote(mine, mine, x_s.at[4, t], x_r.at[4, t], xm),
            remote(mine, mine, x_s.at[5, t], x_r.at[5, t], xp),
        )

    def ag2(t):
        up = tt.at[t, part(low, 0, H)]
        down = tt.at[t, part(high, H, H)]
        return (
            remote(down, down, x_s.at[6, t], x_r.at[6, t], xm),
            remote(up, up, x_s.at[7, t], x_r.at[7, t], xp),
        )

    def start(copies):
        for copy in copies:
            copy.start()

    def wait_recv(copies):
        for copy in copies:
            copy.wait_recv()

    @pl.when(cross)
    def _():
        for k in range(K):
            in_remote(k).start()

    @pl.when(straight)
    def _():
        for k in range(K):
            in_local(k).start()

    def forward(k):
        @pl.when(cross)
        def _():
            in_remote(k).wait_recv()

        @pl.when(straight)
        def _():
            in_local(k).wait()

        z_in(k).start()

    def spread(k):
        z_in(k).wait_recv()
        c_in(k).start()

    def nt(a, b):
        return lax.dot_general(a, b, (((1,), (1,)), ((), ())), preferred_element_type=F32)

    def tn(a, b):
        return lax.dot_general(a, b, (((0,), (0,)), ((), ())), preferred_element_type=F32)

    def nn(a, b):
        return lax.dot_general(a, b, (((1,), (0,)), ((), ())), preferred_element_type=F32)

    def stage_a(t):
        a, b = TILES[t]
        slot = t % SLOTS
        for half in (0, 1):
            vf[slot, :, half * R : (half + 1) * R] = nt(bi[a], bp[half, b])
        s1[t] = vf[slot, part(far, 0, S), :].astype(BF16)
        start(rs1(t))

    def stage_b(t):
        slot = t % SLOTS
        wait_recv(rs1(t))
        s2[t, 0, 0:H] = (vf[slot, part(low, 0, H), :] + r1[t, 0].astype(F32)).astype(BF16)
        s2[t, 0, H:S] = vf[slot, part(low, H, H), :].astype(BF16)
        s2[t, 1, 0:H] = vf[slot, part(high, 0, H), :].astype(BF16)
        s2[t, 1, H:S] = (vf[slot, part(high, H, H), :] + r1[t, 1].astype(F32)).astype(BF16)
        start(rs2(t))

    def stage_c(t):
        a, b = TILES[t]
        slot = t % SLOTS
        wait_recv(rs2(t))
        total = vf[slot, part(x, 0, S), :] + r2[t, 0].astype(F32) + r2[t, 1].astype(F32)
        level = acol_ref[pl.ds(pl.multiple_of(a * R + x * S, S), S), :]
        for half in (0, 1):
            cols = slice(half * R, (half + 1) * R)
            gap = level - brow_ref[half : half + 1, b * R : (b + 1) * R]
            tt[t, part(x, 0, S), cols] = (total[:, cols] / gap).astype(BF16)
        start(ag1(t))

    def stage_d(t):
        wait_recv(ag1(t))
        start(ag2(t))

    def stage_e(t):
        a, b = TILES[t]
        wait_recv(ag2(t))
        first_row = all(tile[0] != a for tile in TILES[:t])
        first_col = all(tile[1] != b for tile in TILES[:t])
        for half in (0, 1):
            term = tn(tt[t, :, half * R : (half + 1) * R], bi[a])
            if first_col:
                back[half, b] = term
            else:
                back[half, b] += term
        if COL_END[b] == t:
            c_back(b).start()
        term = nn(tt[t, :, 0:R], bp[0, b]) + nn(tt[t, :, R:W], bp[1, b])
        if first_row:
            own[a] = term
        else:
            own[a] += term

    def stage_f(k):
        c_back(k).wait_recv()
        zs[k] = (back[0, k] + cr[k]).astype(BF16)
        z_back(k).start()

    def stage_g(k):
        z_back(k).wait_recv()
        os_[k] = (own[k] + zr[k].astype(F32)).astype(BF16)

        @pl.when(cross)
        def _():
            out_remote(k).start()

        @pl.when(straight)
        def _():
            out_local(k).start()

    arrived = set()
    sent = 0
    last = NT + OFF["E"] + 6
    done_f, done_g = set(), set()
    for it in range(last):
        for k in range(K):
            if k not in done_f and it - OFF["E"] > COL_END[k]:
                stage_f(k)
                done_f.add(k)
        for k in range(K):
            if k not in done_g and k in done_f and it - OFF["E"] > max(COL_END[k] + 2, ROW_END[k]):
                stage_g(k)
                done_g.add(k)
        for name, stage in (("E", stage_e), ("D", stage_d), ("C", stage_c), ("B", stage_b)):
            t = it - OFF[name]
            if 0 <= t < NT:
                stage(t)
        if it < NT:
            a, b = TILES[it]
            while sent <= min(K - 1, max(a, b) + 1):
                if sent > 0 and sent - 1 not in arrived:
                    spread(sent - 1)
                    arrived.add(sent - 1)
                    pending = sent - 1
                else:
                    pending = None
                forward(sent)
                if pending is not None:
                    c_in(pending).wait_recv()
                sent += 1
            for k in (a, b):
                if k not in arrived:
                    spread(k)
                    c_in(k).wait_recv()
                    arrived.add(k)
            stage_a(it)

    for t in range(NT):
        for group in (rs1(t), rs2(t), ag1(t), ag2(t)):
            for copy in group:
                copy.wait_send()
    for k in range(K):
        z_in(k).wait_send()
        c_in(k).wait_send()
        c_back(k).wait_send()
        z_back(k).wait_send()

    @pl.when(cross)
    def _():
        for k in range(K):
            in_remote(k).wait_send()
            out_remote(k).wait()

    @pl.when(straight)
    def _():
        for k in range(K):
            out_local(k).wait()


def on_device(integrals, occ_energy, vir_energy):
    o, v = lax.axis_index("occ"), lax.axis_index("vir")
    core = lax.rem(o, 2)
    i = o - core + v
    level = lax.dynamic_slice_in_dim(occ_energy, i, 1) + lax.dynamic_slice_in_dim(
        occ_energy, lax.rem(i + 30, 32), 1
    )
    halves = vir_energy.reshape(2, 1024)
    mine = lax.dynamic_slice_in_dim(vir_energy, core * 1024, 1024)
    other = lax.dynamic_slice_in_dim(vir_energy, (1 - core) * 1024, 1024)
    acol = (level - mine)[:, None]
    brow = jnp.stack([mine, other])
    dma = pltpu.SemaphoreType.DMA
    vmem = pltpu.VMEM
    out = pl.pallas_call(
        kernel,
        out_shape=jax.ShapeDtypeStruct((1024, 1024), BF16),
        in_specs=[
            pl.BlockSpec(memory_space=pl.ANY),
            pl.BlockSpec(memory_space=pltpu.VMEM),
            pl.BlockSpec(memory_space=pltpu.VMEM),
        ],
        out_specs=pl.BlockSpec(memory_space=pl.ANY),
        scratch_shapes=[
            vmem((K, R, 1024), BF16),
            vmem((2, K, R, 1024), BF16),
            vmem((SLOTS, R, W), F32),
            vmem((NT, S, W), BF16),
            vmem((NT, 2, S, W), BF16),
            vmem((NT, 2, H, W), BF16),
            vmem((NT, 2, S, W), BF16),
            vmem((NT, R, W), BF16),
            vmem((K, R, 1024), F32),
            vmem((2, K, R, 1024), F32),
            vmem((K, R, 1024), F32),
            vmem((K, R, 1024), BF16),
            vmem((K, R, 1024), BF16),
            vmem((K, R, 1024), BF16),
            dma((K,)), dma((K,)), dma((K,)), dma((K,)), dma((K,)), dma((K,)),
            dma((8, NT)), dma((8, NT)),
            dma((K,)), dma((K,)), dma((K,)), dma((K,)), dma((K,)), dma((K,)),
        ],
        compiler_params=pltpu.CompilerParams(
            collective_id=0, has_side_effects=True, vmem_limit_bytes=58 * 2**20
        ),
        cost_estimate=pl.CostEstimate(flops=13 * 10**9, bytes_accessed=4 * 2**20, transcendentals=0),
        name="pair_lagrangian",
    )(integrals.reshape(1024, 1024), acol, brow)
    return out.reshape(1, 1024, 1024)


def solution(mesh):
    placed = (P("occ", "vir", "aux"), P(), P())
    return jax.shard_map(
        on_device, mesh=mesh, in_specs=placed, out_specs=P("occ", "vir", "aux"), check_vma=False
    )
```

time: 495 us -> 214 us (0.43)
  waiting for transfers between devices: 442 us -> 0 us
  Pallas kernels: 0 us -> 206 us
  matrix products: 29 us -> 0 us
  between operations: 14.5 us -> 1.3 us
    pallas_call x0 -> x1, Pallas kernels: none -> 206 us  [on_device(): pl.pallas_call(kernel, out_shape=jax.ShapeDtypeStruct((1024, 1024), BF16)...]
    reduce_scatter x2 -> x0, waiting for transfers between devices: 186 us -> none  [the longest x1 106 us: on_device(): lax.psum_scatter(second_part, 'vir', scatter_dimension=1, tiled=True)]
    ppermute x2 -> x0, waiting for transfers between devices: 139 us -> none  [shifted_2(): lax.ppermute(value, axis, [(i, (i + by) % count) for i in range(count)])]
    all_gather x2 -> x0, waiting for transfers between devices: 117 us -> none  [the longest x1 66 us: on_device(): partner = lax.all_gather(shifted, 'vir', axis=1, tiled=True)]
    dot_general x3 -> x0, matrix products: 29 us -> none  [the longest x1 10.6 us: on_device(): jnp.einsum('nbq,naq->bna', partner_cols, integrals, preferred_element_typ...]
  transfers between devices with their start and end apart: 6 -> 0, of which waited for: 6 -> 0; matrix products, arithmetic and copies ran while one was open for 0% -> 0% of each run, Pallas kernels for 0% -> 0%
where the time goes in v1:
time: 214 us
  Pallas kernels  206 us (96%)
  local copies, waits for them, and re-layouts  5.45 us (3%)
    pallas_call x1, Pallas kernels, on_device(): pl.pallas_call(kernel, out_shape=jax.ShapeDtypeStruct((1024, 1024), BF16)...  206 us

profile of v1, /device:TPU:225, one launch (start us, length us, event | category | flops | bytes accessed | tf_op | source)
XLA Modules:
  0.0 214.2 jit_solution(6539293866990456413)
XLA Ops:
  0.0 1.3 fusion
  2.6 0.7 broadcast_subtract_fusion
  3.3 0.6 pad_maximum_fusion.brow_ref
  4.0 1.0 copy.4.acol_ref
  5.0 206.1 %pair_lagrangian.1 = bf16[1024,1024]{1,0:T(8,128)(2,1)} custom-call(bf16[1024,1024]{1,0:T(8,128)(2,1)} %bitcast.10, f32[1024,1]{1,0:T(8,128)} %copy.4.acol_ref, f32[2,1024]{1,0:T(2,128)} %pad_maximum_fusion.brow_ref), custom_call_target="tpu_custom_call" | custom-call | flops 12999999488 | bytes 4194304 | tf_op jit(solution)/shard_map/pair_lagrangian/pallas_call | solution.py:305
  211.1 3.1 %copy.6 = bf16[1,1024,1024]{2,1,0:T(8,128)(2,1)} copy(bf16[1,1024,1024]{2,1,0:T(8,128)(2,1)} %bitcast.6) | data formatting | bytes 4194304

commit v2 on v1

v2 whole, which is shorter than its diff:
```python
import functools

import jax
import jax.numpy as jnp
from jax import lax
from jax.experimental import pallas as pl
from jax.experimental.pallas import tpu as pltpu
from jax.sharding import PartitionSpec as P

MESH = pl.DeviceIdType.MESH
BF16 = jnp.bfloat16
F32 = jnp.float32

N = 1024
R = 256
S = R // 4
H = S // 2
SLOTS = 6

SIZES = [128, 128, 256, 256, 128, 128]
K = len(SIZES)
START = [sum(SIZES[:k]) for k in range(K)]
ROWS = N // R
NEEDS = [[k for k in range(K) if START[k] // R == a] for a in range(ROWS)]

TILES = [(0, 0), (1, 0), (0, 1), (1, 1), (2, 0), (2, 1), (3, 0), (3, 1)]
TILES += [(a, b) for b in range(2, K) for a in range(ROWS)]
NT = len(TILES)
WIDE = max(SIZES)
KIND = [0 if SIZES[b] == WIDE else 1 for a, b in TILES]
PLACE = [KIND[:t].count(KIND[t]) for t in range(NT)]
COUNT = [KIND.count(0), KIND.count(1)]
ROW_END = [max(t for t, tile in enumerate(TILES) if tile[0] == a) for a in range(ROWS)]
COL_END = [max(t for t, tile in enumerate(TILES) if tile[1] == b) for b in range(K)]

OFF = {"A": 0, "B": 2, "C": 4, "D": 6, "E": 7}
FORWARD = {0: [0, 1], 1: [2], 2: [3], 4: [4], 5: [5]}
DIRECT = {0: [0, 1], 4: [2], 6: [3], 8: [4], 10: [5]}
SPREAD = {0: [0], 2: [1], 5: [2], 9: [3], 12: [4], 14: [5]}


def kernel(
    x_ref, occ_ref, vir_ref, out_ref,
    bi, bp, acol, vf, s1w, s1n, s2w, s2n, r1w, r1n, r2w, r2n, ttw, ttn, own, back, cr, zs, zr, os_, ow, os2,
    in_s, in_r, zi_s, zi_r, ci_s, ci_r, x_s, x_r, cb_s, cb_r, zb_s, zb_r, o_s, o_r, w_s, w_r,
):
    o, x, v = lax.axis_index("occ"), lax.axis_index("aux"), lax.axis_index("vir")
    c = lax.rem(o, 2)
    base = o - c
    z = lax.rem(o, 16) // 2
    last = z // 7
    first = 1 - (z + 7) // 8
    cross = c + v == 1
    straight = c + v != 1
    cross_last = lax.rem(c + v, 2) + last == 2
    cross_inner = lax.rem(c + v, 2) - last == 1
    xp = (o, lax.rem(x + 1, 4), v)
    xm = (o, lax.rem(x + 3, 4), v)
    zp = (lax.rem(base + 2, 32) + c + last * (v - c), x, v + last * (c - v))
    zm = (lax.rem(base + 30, 32) + c + first * (v - c), x, v + first * (c - v))
    core = (base + 1 - c, x, v)
    swap = (base + 1 - c, x, 1 - v)
    s1, s2, r1, r2, tt = (s1w, s1n), (s2w, s2n), (r1w, r1n), (r2w, r2n), (ttw, ttn)

    def remote(src, dst, ssem, rsem, to):
        return pltpu.make_async_remote_copy(
            src_ref=src, dst_ref=dst, send_sem=ssem, recv_sem=rsem, device_id=to, device_id_type=MESH
        )

    barrier = pltpu.get_barrier_semaphore()
    for peer in (xp, xm, zp, zm, core, swap):
        pl.semaphore_signal(barrier, inc=1, device_id=peer, device_id_type=MESH)
    pl.semaphore_wait(barrier, 6)

    def rows(k):
        return pl.ds(START[k], SIZES[k])

    def pair(k, half):
        return pl.ds(2 * START[k] + half * SIZES[k], SIZES[k])

    def in_remote(k):
        return remote(x_ref.at[rows(k)], bi.at[rows(k)], in_s.at[k], in_r.at[k], swap)

    def in_local(k):
        return pltpu.make_async_copy(x_ref.at[rows(k)], bi.at[rows(k)], in_r.at[k])

    def z_in(k):
        return remote(bi.at[rows(k)], bp.at[pair(k, 0)], zi_s.at[k], zi_r.at[k], zp)

    def z_direct(k):
        return remote(x_ref.at[rows(k)], bp.at[pair(k, 0)], zi_s.at[k], zi_r.at[k], zp)

    def c_in(k):
        return remote(bp.at[pair(k, 0)], bp.at[pair(k, 1)], ci_s.at[k], ci_r.at[k], core)

    def c_back(k):
        return remote(back.at[pair(k, 1)], cr.at[rows(k)], cb_s.at[k], cb_r.at[k], core)

    def z_back(k):
        return remote(zs.at[rows(k)], zr.at[rows(k)], zb_s.at[k], zb_r.at[k], zm)

    def out_remote(k):
        return remote(os_.at[rows(k)], out_ref.at[rows(k)], o_s.at[k], o_r.at[k], swap)

    def out_local(k):
        return pltpu.make_async_copy(os_.at[rows(k)], out_ref.at[rows(k)], o_r.at[k])

    def own_remote(k):
        return remote(os_.at[rows(k)], ow.at[rows(k)], w_s.at[k], w_r.at[k], swap)

    def out_sum(k):
        return pltpu.make_async_copy(os2.at[rows(k)], out_ref.at[rows(k)], o_r.at[k])

    far = lax.rem(x + 2, 4)
    low = lax.rem(x + 3, 4)
    high = lax.rem(x + 1, 4)

    def part(shard, begin, count):
        return pl.ds(pl.multiple_of(shard * S + begin, H), count)

    def of(refs, t):
        return refs[KIND[t]].at[PLACE[t]]

    def rs1(t):
        src, dst = of(s1, t), of(r1, t)
        return (
            remote(src.at[pl.ds(0, H)], dst.at[0], x_s.at[0, t], x_r.at[0, t], xm),
            remote(src.at[pl.ds(H, H)], dst.at[1], x_s.at[1, t], x_r.at[1, t], xp),
        )

    def rs2(t):
        src, dst = of(s2, t), of(r2, t)
        return (
            remote(src.at[0], dst.at[0], x_s.at[2, t], x_r.at[2, t], xm),
            remote(src.at[1], dst.at[1], x_s.at[3, t], x_r.at[3, t], xp),
        )

    def ag1(t):
        mine = of(tt, t).at[part(x, 0, S)]
        return (
            remote(mine, mine, x_s.at[4, t], x_r.at[4, t], xm),
            remote(mine, mine, x_s.at[5, t], x_r.at[5, t], xp),
        )

    def ag2(t):
        up = of(tt, t).at[part(low, 0, H)]
        down = of(tt, t).at[part(high, H, H)]
        return (
            remote(down, down, x_s.at[6, t], x_r.at[6, t], xm),
            remote(up, up, x_s.at[7, t], x_r.at[7, t], xp),
        )

    def start(copies):
        for copy in copies:
            copy.start()

    def wait_recv(copies):
        for copy in copies:
            copy.wait_recv()

    for k in range(K):
        @pl.when(cross)
        def _():
            in_remote(k).start()

        @pl.when(straight)
        def _():
            in_local(k).start()

    def direct(k):
        @pl.when(last == 1)
        def _():
            z_direct(k).start()

    def forward(k):
        @pl.when(cross)
        def _():
            in_remote(k).wait_recv()

        @pl.when(straight)
        def _():
            in_local(k).wait()

        @pl.when(last == 0)
        def _():
            z_in(k).start()

    def spread(k):
        z_in(k).wait_recv()
        c_in(k).start()

    def dot(a, b, over):
        return lax.dot_general(a, b, ((over[:1], over[1:]), ((), ())), preferred_element_type=F32)

    level = occ_ref[base + v] + occ_ref[lax.rem(base + v + 30, 32)]
    for j in range(N // 128):
        lanes = pl.ds(pl.multiple_of(c * N + j * 128, 128), 128)
        acol[j * 128 : (j + 1) * 128, :] = jnp.broadcast_to(level - vir_ref[0:1, lanes], (128, 128)).T

    def stage_a(t):
        a, b = TILES[t]
        width = 2 * SIZES[b]
        slot = t % SLOTS
        vf[slot, :, 0:width] = dot(
            bi[a * R : (a + 1) * R], bp[2 * START[b] : 2 * START[b] + width], (1, 1)
        )
        of(s1, t)[...] = vf[slot, part(far, 0, S), 0:width].astype(BF16)
        start(rs1(t))

    def stage_b(t):
        slot = t % SLOTS
        width = 2 * SIZES[TILES[t][1]]
        wait_recv(rs1(t))
        got, put = of(r1, t), of(s2, t)
        put[0, 0:H] = (vf[slot, part(low, 0, H), 0:width] + got[0].astype(F32)).astype(BF16)
        put[0, H:S] = vf[slot, part(low, H, H), 0:width].astype(BF16)
        put[1, 0:H] = vf[slot, part(high, 0, H), 0:width].astype(BF16)
        put[1, H:S] = (vf[slot, part(high, H, H), 0:width] + got[1].astype(F32)).astype(BF16)
        start(rs2(t))

    def stage_c(t):
        a, b = TILES[t]
        size = SIZES[b]
        slot = t % SLOTS
        wait_recv(rs2(t))
        got, put = of(r2, t), of(tt, t)
        level_a = acol[pl.ds(pl.multiple_of(a * R + x * S, S), S), 0:1]
        for half in (0, 1):
            cols = slice(half * size, (half + 1) * size)
            total = vf[slot, part(x, 0, S), cols] + got[0, :, cols].astype(F32) + got[1, :, cols].astype(F32)
            begin = (c + half - 2 * c * half) * N + START[b]
            gap = level_a - vir_ref[0:1, pl.ds(pl.multiple_of(begin, 128), size)]
            put[part(x, 0, S), cols] = (total / gap).astype(BF16)
        start(ag1(t))

    def stage_d(t):
        wait_recv(ag1(t))
        start(ag2(t))

    def stage_e(t):
        a, b = TILES[t]
        wait_recv(ag2(t))
        own_rows = slice(a * R, (a + 1) * R)
        pair_rows = slice(2 * START[b], 2 * START[b] + 2 * SIZES[b])
        tile = of(tt, t)[...]
        term = dot(tile, bi[own_rows], (0, 0))
        if all(other[1] != b for other in TILES[:t]):
            back[pair_rows] = term
        else:
            back[pair_rows] += term
        if COL_END[b] == t:
            c_back(b).start()
        term = dot(tile, bp[pair_rows], (1, 0))
        if all(other[0] != a for other in TILES[:t]):
            own[own_rows] = term
        else:
            own[own_rows] += term

    def stage_f(k):
        r = slice(START[k], START[k] + SIZES[k])
        c_back(k).wait_recv()
        zs[r] = (back[2 * START[k] : 2 * START[k] + SIZES[k]] + cr[r]).astype(BF16)
        z_back(k).start()

    def stage_g(k):
        r = slice(START[k], START[k] + SIZES[k])

        @pl.when(cross_last)
        def _():
            os_[r] = own[r].astype(BF16)
            own_remote(k).start()

        @pl.when(lax.rem(c + v, 2) + last != 2)
        def _():
            z_back(k).wait_recv()
            os_[r] = (own[r] + zr[r].astype(F32)).astype(BF16)

            @pl.when(cross)
            def _():
                out_remote(k).start()

            @pl.when(straight)
            def _():
                out_local(k).start()

    def stage_h(k):
        r = slice(START[k], START[k] + SIZES[k])

        @pl.when(cross_last)
        def _():
            own_remote(k).wait_recv()
            z_back(k).wait_recv()
            os2[r] = (ow[r].astype(F32) + zr[r].astype(F32)).astype(BF16)
            out_sum(k).start()

    done_f, done_g = set(), set()
    for it in range(NT + OFF["E"] + 1):
        for name, stage in (("D", stage_d), ("C", stage_c), ("B", stage_b)):
            t = it - OFF[name]
            if 0 <= t < NT:
                stage(t)
        if it < NT:
            a, b = TILES[it]
            for k in DIRECT.get(it, []):
                direct(k)
            for k in FORWARD.get(it, []):
                forward(k)
            for k in SPREAD.get(it, []):
                spread(k)
            if all(other[1] != b for other in TILES[:it]):
                c_in(b).wait_recv()
            stage_a(it)
        t = it - OFF["E"]
        for k in range(K):
            if k not in done_f and t > COL_END[k]:
                stage_f(k)
                done_f.add(k)
        if 0 <= t < NT:
            stage_e(t)
        for k in range(K):
            if k not in done_g and COL_END[k] + 3 <= t and ROW_END[START[k] // R] <= t:
                stage_g(k)
                done_g.add(k)
    for k in range(K):
        if k not in done_f:
            stage_f(k)
    for k in range(K):
        if k not in done_g:
            stage_g(k)
    for k in range(K):
        stage_h(k)

    for t in range(NT):
        for group in (rs1(t), rs2(t), ag1(t), ag2(t)):
            for copy in group:
                copy.wait_send()
    for k in range(K):
        @pl.when(last == 0)
        def _():
            z_in(k).wait_send()

        @pl.when(last == 1)
        def _():
            z_direct(k).wait_send()

        c_in(k).wait_send()
        c_back(k).wait_send()
        z_back(k).wait_send()

        @pl.when(cross)
        def _():
            in_remote(k).wait_send()

        @pl.when(cross_inner)
        def _():
            out_remote(k).wait()

        @pl.when(cross_last)
        def _():
            own_remote(k).wait_send()
            out_sum(k).wait()

        @pl.when(straight)
        def _():
            out_local(k).wait()


def on_device(integrals, occ_energy, vir_energy):
    dma = pltpu.SemaphoreType.DMA
    vmem = pltpu.VMEM

    def tiles(*lead):
        return [vmem((COUNT[kind], *lead, 2 * (WIDE >> kind)), BF16) for kind in (0, 1)]

    out = pl.pallas_call(
        kernel,
        out_shape=jax.ShapeDtypeStruct((N, N), BF16),
        in_specs=[
            pl.BlockSpec(memory_space=pl.ANY),
            pl.BlockSpec(memory_space=pltpu.SMEM),
            pl.BlockSpec(memory_space=pltpu.VMEM),
        ],
        out_specs=pl.BlockSpec(memory_space=pl.ANY),
        scratch_shapes=[
            vmem((N, N), BF16),
            vmem((2 * N, N), BF16),
            vmem((N, 128), F32),
            vmem((SLOTS, R, 2 * WIDE), F32),
            *tiles(S),
            *tiles(2, S),
            *tiles(2, H),
            *tiles(2, S),
            *tiles(R),
            vmem((N, N), F32),
            vmem((2 * N, N), F32),
            vmem((N, N), F32),
            vmem((N, N), BF16),
            vmem((N, N), BF16),
            vmem((N, N), BF16),
            vmem((N, N), BF16),
            vmem((N, N), BF16),
            *[dma((K,))] * 6,
            dma((8, NT)), dma((8, NT)),
            *[dma((K,))] * 8,
        ],
        compiler_params=pltpu.CompilerParams(
            collective_id=0, has_side_effects=True, vmem_limit_bytes=58 * 2**20
        ),
        cost_estimate=pl.CostEstimate(flops=13 * 10**9, bytes_accessed=4 * 2**20, transcendentals=0),
        name="pair_lagrangian",
    )(integrals.reshape(N, N), occ_energy, vir_energy.reshape(1, 2 * N))
    return out.reshape(1, N, N)


def solution(mesh):
    placed = (P("occ", "vir", "aux"), P(), P())
    return jax.shard_map(
        on_device, mesh=mesh, in_specs=placed, out_specs=P("occ", "vir", "aux"), check_vma=False
    )
```

time: 214 us -> 148 us (0.69); the launches traced: 214 us -> 145 us
  Pallas kernels: 206 us -> 142 us
  local copies, waits for them, and re-layouts: 5.45 us -> 3.08 us
    pallas_call x1, Pallas kernels: 206 us -> 142 us  [on_device(): pl.pallas_call(kernel, out_shape=jax.ShapeDtypeStruct((N, N), BF16), in_s...]
where the time goes in v2:
time: 148 us; the launch traced here: 145 us
  Pallas kernels  142 us (96%)
  local copies, waits for them, and re-layouts  3.08 us (2%)
    pallas_call x1, Pallas kernels, on_device(): pl.pallas_call(kernel, out_shape=jax.ShapeDtypeStruct((N, N), BF16), in_s...  142 us
    unnamed x1, local copies, waits for them, and re-layouts  3.08 us

profile of v2, /device:TPU:225, one launch (start us, length us, event | category | flops | bytes accessed | tf_op | source)
XLA Modules:
  0.0 145.2 jit_solution(7032173271239532912)
XLA Ops:
  0.0 142.1 %pair_lagrangian.1 = bf16[1024,1024]{1,0:T(8,128)(2,1)} custom-call(bf16[1024,1024]{1,0:T(8,128)(2,1)} %bitcast.4, f32[32]{0:T(128)} %occ_ref.1, f32[1,2048]{1,0:T(1,128)} %bitcast.5), custom_call_target="tpu_custom_call" | custom-call | flops 12999999488 | bytes 4194304 | tf_op jit(solution)/shard_map/pair_lagrangian/pallas_call | solution.py:375
  142.2 3.1 %copy.5 = bf16[1,1024,1024]{2,1,0:T(8,128)(2,1)} copy(bf16[1,1024,1024]{2,1,0:T(8,128)(2,1)} %bitcast.3) | data formatting | bytes 4194304

commit v3 on v2

--- a/solution.py
+++ b/solution.py
@@ -23,8 +23,8 @@
 ROWS = N // R
 NEEDS = [[k for k in range(K) if START[k] // R == a] for a in range(ROWS)]
 
-TILES = [(0, 0), (1, 0), (0, 1), (1, 1), (2, 0), (2, 1), (3, 0), (3, 1)]
-TILES += [(a, b) for b in range(2, K) for a in range(ROWS)]
+TILES = [(0, 0), (1, 0), (0, 1), (1, 1), (2, 0), (2, 1), (0, 2), (1, 2), (3, 0), (3, 1), (2, 2), (3, 2)]
+TILES += [(a, 3) for a in range(ROWS)] + [(0, 4), (0, 5), (1, 4), (1, 5), (2, 4), (3, 4), (2, 5), (3, 5)]
 NT = len(TILES)
 WIDE = max(SIZES)
 KIND = [0 if SIZES[b] == WIDE else 1 for a, b in TILES]
@@ -34,8 +34,8 @@
 COL_END = [max(t for t, tile in enumerate(TILES) if tile[1] == b) for b in range(K)]
 
 OFF = {"A": 0, "B": 2, "C": 4, "D": 6, "E": 7}
-FORWARD = {0: [0, 1], 1: [2], 2: [3], 4: [4], 5: [5]}
-DIRECT = {0: [0, 1], 4: [2], 6: [3], 8: [4], 10: [5]}
+FORWARD = {0: [0, 1], 1: [2], 3: [3], 5: [4], 6: [5]}
+DIRECT = {3: [2], 6: [3], 8: [4], 10: [5]}
 SPREAD = {0: [0], 2: [1], 5: [2], 9: [3], 12: [4], 14: [5]}
 
 
@@ -52,6 +52,7 @@
     first = 1 - (z + 7) // 8
     cross = c + v == 1
     straight = c + v != 1
+    straight_last = last - lax.rem(c + v, 2) == 1
     cross_last = lax.rem(c + v, 2) + last == 2
     cross_inner = lax.rem(c + v, 2) - last == 1
     xp = (o, lax.rem(x + 1, 4), v)
@@ -158,6 +159,11 @@
         for copy in copies:
             copy.wait_recv()
 
+    def direct(k):
+        @pl.when(last == 1)
+        def _():
+            z_direct(k).start()
+
     for k in range(K):
         @pl.when(cross)
         def _():
@@ -167,10 +173,8 @@
         def _():
             in_local(k).start()
 
-    def direct(k):
-        @pl.when(last == 1)
-        def _():
-            z_direct(k).start()
+        if k < 2:
+            direct(k)
 
     def forward(k):
         @pl.when(cross)
@@ -270,7 +274,7 @@
             os_[r] = own[r].astype(BF16)
             own_remote(k).start()
 
-        @pl.when(lax.rem(c + v, 2) + last != 2)
+        @pl.when(last == 0)
         def _():
             z_back(k).wait_recv()
             os_[r] = (own[r] + zr[r].astype(F32)).astype(BF16)
@@ -293,8 +297,14 @@
             os2[r] = (ow[r].astype(F32) + zr[r].astype(F32)).astype(BF16)
             out_sum(k).start()
 
-    done_f, done_g = set(), set()
-    for it in range(NT + OFF["E"] + 1):
+        @pl.when(straight_last)
+        def _():
+            z_back(k).wait_recv()
+            os_[r] = (own[r] + zr[r].astype(F32)).astype(BF16)
+            out_local(k).start()
+
+    done_f, done_g, done_h = set(), {}, set()
+    for it in range(NT + OFF["E"]):
         for name, stage in (("D", stage_d), ("C", stage_c), ("B", stage_b)):
             t = it - OFF[name]
             if 0 <= t < NT:
@@ -320,7 +330,7 @@
         for k in range(K):
             if k not in done_g and COL_END[k] + 3 <= t and ROW_END[START[k] // R] <= t:
                 stage_g(k)
-                done_g.add(k)
+                done_g[k] = t
     for k in range(K):
         if k not in done_f:
             stage_f(k)
@@ -328,7 +338,8 @@
         if k not in done_g:
             stage_g(k)
     for k in range(K):
-        stage_h(k)
+        if k not in done_h:
+            stage_h(k)
 
     for t in range(NT):
         for group in (rs1(t), rs2(t), ag1(t), ag2(t)):

time: 148 us -> 141 us (0.953); the launches traced: 145 us -> 141 us
  Pallas kernels: 142 us -> 138 us
    pallas_call x1, Pallas kernels: 142 us -> 138 us  [on_device(): pl.pallas_call(kernel, out_shape=jax.ShapeDtypeStruct((N, N), BF16), in_s...]
where the time goes in v3:
time: 141 us
  Pallas kernels  138 us (98%)
  local copies, waits for them, and re-layouts  3.08 us (2%)
    pallas_call x1, Pallas kernels, on_device(): pl.pallas_call(kernel, out_shape=jax.ShapeDtypeStruct((N, N), BF16), in_s...  138 us
    unnamed x1, local copies, waits for them, and re-layouts  3.08 us

profile of v3, /device:TPU:225, one launch (start us, length us, event | category | flops | bytes accessed | tf_op | source)
XLA Modules:
  0.0 141.1 jit_solution(14216450276026881556)
XLA Ops:
  0.0 138.0 %pair_lagrangian.1 = bf16[1024,1024]{1,0:T(8,128)(2,1)} custom-call(bf16[1024,1024]{1,0:T(8,128)(2,1)} %bitcast.4, f32[32]{0:T(128)} %occ_ref.1, f32[1,2048]{1,0:T(1,128)} %bitcast.5), custom_call_target="tpu_custom_call" | custom-call | flops 12999999488 | bytes 4194304 | tf_op jit(solution)/shard_map/pair_lagrangian/pallas_call | solution.py:386
  138.1 3.1 %copy.5 = bf16[1,1024,1024]{2,1,0:T(8,128)(2,1)} copy(bf16[1,1024,1024]{2,1,0:T(8,128)(2,1)} %bitcast.3) | data formatting | bytes 4194304

commit v4 on v3

--- a/solution.py
+++ b/solution.py
@@ -33,7 +33,7 @@
 ROW_END = [max(t for t, tile in enumerate(TILES) if tile[0] == a) for a in range(ROWS)]
 COL_END = [max(t for t, tile in enumerate(TILES) if tile[1] == b) for b in range(K)]
 
-OFF = {"A": 0, "B": 2, "C": 4, "D": 6, "E": 7}
+OFF = {"A": 0, "B": 2, "C": 5, "D": 7, "E": 8}
 FORWARD = {0: [0, 1], 1: [2], 3: [3], 5: [4], 6: [5]}
 DIRECT = {3: [2], 6: [3], 8: [4], 10: [5]}
 SPREAD = {0: [0], 2: [1], 5: [2], 9: [3], 12: [4], 14: [5]}

time: 141 us -> 143 us (1.014)
  Pallas kernels: 138 us -> 140 us
    pallas_call x1, Pallas kernels: 138 us -> 140 us  [on_device(): pl.pallas_call(kernel, out_shape=jax.ShapeDtypeStruct((N, N), BF16), in_s...]
where the time goes in v4:
time: 143 us
  Pallas kernels  140 us (98%)
  local copies, waits for them, and re-layouts  3.08 us (2%)
    pallas_call x1, Pallas kernels, on_device(): pl.pallas_call(kernel, out_shape=jax.ShapeDtypeStruct((N, N), BF16), in_s...  140 us
    unnamed x1, local copies, waits for them, and re-layouts  3.08 us

profile of v4, /device:TPU:225, one launch (start us, length us, event | category | flops | bytes accessed | tf_op | source)
XLA Modules:
  0.0 142.9 jit_solution(4401219734679708988)
XLA Ops:
  0.0 139.8 %pair_lagrangian.1 = bf16[1024,1024]{1,0:T(8,128)(2,1)} custom-call(bf16[1024,1024]{1,0:T(8,128)(2,1)} %bitcast.4, f32[32]{0:T(128)} %occ_ref.1, f32[1,2048]{1,0:T(1,128)} %bitcast.5), custom_call_target="tpu_custom_call" | custom-call | flops 12999999488 | bytes 4194304 | tf_op jit(solution)/shard_map/pair_lagrangian/pallas_call | solution.py:386
  139.8 3.1 %copy.5 = bf16[1,1024,1024]{2,1,0:T(8,128)(2,1)} copy(bf16[1,1024,1024]{2,1,0:T(8,128)(2,1)} %bitcast.3) | data formatting | bytes 4194304
